TPU v7x, 32 devices: a whole 2x2x4 slice. The times are simulated.
32 devices in a mesh: dp: 8 (over z, core), vocab: 4 (over y, x).
Axes of the slice: x: 2, y: 2, z: 4, core: 2. Of those that a mesh axis runs over, the one named last changes fastest.
Arguments:
- hidden: bfloat16 [2048, 4096], P('dp')
- table: bfloat16 [16384, 4096], P(('vocab', 'dp')), as said below
- targets: int32 [2048], P('dp'), may hold values from 0 to 16383
- token_scale: float32 [2048], P('dp'), may hold values from 2 to 32
- enc_ids: int32 [512], P(('dp', 'vocab')), may hold values from 0 to 16383
- enc_cot: bfloat16 [512, 4096], P(('dp', 'vocab')), may hold values from -6 to 6
- dec_ids: int32 [512], P(('dp', 'vocab')), may hold values from 0 to 16383
- dec_cot: bfloat16 [512, 4096], P(('dp', 'vocab')), may hold values from -6 to 6
Outputs:
- grad_hidden: bfloat16 [2048, 4096], P('dp', 'vocab')
- grad_table: float32 [16384, 4096], P(('vocab', 'dp'))
- loss: float32 [2048], P('dp')
Inputs may be any that keep to these rules, and one draw needn't show every extreme that they name: table entries of order 3 / sqrt(4096).
All inputs are finite; a program needn't handle non-finite values.
Results may differ from a plain program's by a relative error of at most 0.018.
Values may be sent and summed in bfloat16 or wider, within the bound.
A program may use at most 192 MiB of HBM per device.

v0:
```python
import jax
import jax.numpy as jnp
from jax import lax
from jax.sharding import PartitionSpec as P


def shards(hidden, table, targets, token_scale, enc_ids, enc_cot, dec_ids, dec_cot):
    vocab_rows = table.shape[0] * lax.axis_size("dp")
    offset = lax.axis_index("vocab") * vocab_rows
    gathered = lax.all_gather(table, "dp", axis=0, tiled=True)
    logits = jnp.dot(hidden, gathered.T, preferred_element_type=jnp.float32)
    local_target = targets - offset
    columns = jnp.arange(vocab_rows, dtype=jnp.int32)
    matches = columns[None, :] == local_target[:, None]
    target_part = jnp.sum(jnp.where(matches, logits, 0.0), axis=1)
    local_max = jnp.max(logits, axis=1)
    row_max = lax.pmax(local_max, "vocab")
    expo = jnp.exp(logits - row_max[:, None])
    row_sum, target_logit = lax.psum((jnp.sum(expo, axis=1), target_part), "vocab")
    loss = row_max + jnp.log(row_sum) - target_logit
    dlogits = (
        token_scale[:, None] * (expo / row_sum[:, None] - matches.astype(jnp.float32))
    ).astype(jnp.bfloat16)
    state_term = jnp.dot(dlogits, gathered, preferred_element_type=jnp.float32)
    grad_hidden = lax.psum_scatter(
        state_term.astype(jnp.bfloat16), "vocab", scatter_dimension=1, tiled=True
    )
    ids_one, cot_one, ids_two, cot_two = (
        lax.all_gather(enc_ids, "vocab", axis=0, tiled=True),
        lax.all_gather(enc_cot, "vocab", axis=0, tiled=True),
        lax.all_gather(dec_ids, "vocab", axis=0, tiled=True),
        lax.all_gather(dec_cot, "vocab", axis=0, tiled=True),
    )
    all_ids = jnp.concatenate([ids_one, ids_two], axis=0) - offset
    all_cot = jnp.concatenate([cot_one, cot_two], axis=0)
    hits = (columns[:, None] == all_ids[None, :]).astype(jnp.bfloat16)
    looked_up = jnp.dot(hits, all_cot, preferred_element_type=jnp.float32)
    head = lax.dot_general(
        dlogits, hidden, (((0,), (0,)), ((), ())), preferred_element_type=jnp.float32
    )
    grad_table = lax.psum_scatter(
        (head + looked_up).astype(jnp.bfloat16), "dp", scatter_dimension=0, tiled=True
    ).astype(jnp.float32)
    return (grad_hidden, grad_table, loss)


def solution(mesh):
    placed = (
        P("dp", None),
        P(("vocab", "dp"), None),
        P("dp"),
        P("dp"),
        P(("dp", "vocab")),
        P(("dp", "vocab"), None),
        P(("dp", "vocab")),
        P(("dp", "vocab"), None),
    )
    return jax.shard_map(
        shards,
        mesh=mesh,
        in_specs=placed,
        out_specs=(P("dp", "vocab"), P(("vocab", "dp"), None), P("dp")),
        check_vma=False,
    )
```

profile of v0, /device:TPU:8, one launch (start us, length us, event | category | flops | bytes accessed | tf_op | source)
XLA Modules:
  0.0 764.9 jit_solution(9555794528908825600)
XLA Ops:
  7.2 0.0 copy-start
  7.2 0.0 copy-start.8
  7.2 0.0 copy-start.6
  7.2 0.0 copy-start.7
  7.2 0.0 copy-start.2
  7.2 0.0 copy-start.3
  7.2 0.0 copy-start.5
  7.2 0.0 all-gather.2.cloned.1.call-start
  7.3 0.7 all-gather.2.cloned.1.call-update
  8.0 0.0 reduce-scatter.5.cloned.1.call-start
  8.0 0.0 copy-done.8
  8.0 0.6 dynamic-slice
  9.3 0.0 copy-done.6
  9.3 0.2 dynamic-update-slice.1
  9.5 0.0 copy-done.7
  9.5 0.2 dynamic-update-slice
  9.8 7.4 all-reduce.2
  17.1 0.0 copy-done.2
  17.1 10.3 %all_gather.18 = bf16[64,4096]{1,0:T(8,128)(2,1)S(1)} all-gather(bf16[16,4096]{1,0:T(8,128)(2,1)S(1)} %copy-done.2), channel_id=1, replica_groups=mesh['dp'=8,'vocab'=4] {'vocab'}, dimensions={0}, use_global_device_ids=true | all-gather | bytes 655360 | tf_op jit(solution)/shard_map/all_gather | solution.py:30
  27.5 0.0 copy-done.3
  27.5 9.6 %all_gather.19 = bf16[64,4096]{1,0:T(8,128)(2,1)S(1)} all-gather(bf16[16,4096]{1,0:T(8,128)(2,1)S(1)} %copy-done.3), channel_id=1, replica_groups=mesh['dp'=8,'vocab'=4] {'vocab'}, dimensions={0}, use_global_device_ids=true | all-gather | bytes 655360 | tf_op jit(solution)/shard_map/all_gather | solution.py:32
  37.1 0.1 add_subtract_fusion.1
  37.2 0.0 copy-done.5
  37.2 259.3 %all-gather.2.cloned.1.call-done = bf16[4096,4096]{1,0:T(8,128)(2,1)} async-done(((bf16[512,4096]{1,0:T(8,128)(2,1)}), bf16[4096,4096]{1,0:T(8,128)(2,1)}) %all-gather.2.cloned.1.call-update) | async-done | bytes 33554448 | tf_op jit(solution)/shard_map/all_gather | solution.py:10
  296.5 0.0 copy-done
  296.5 16.4 %fusion.7 = (f32[256]{0:T(256)S(1)}, f32[256,4096]{1,0:T(8,128)}) fusion(bf16[256,4096]{1,0:T(8,128)(2,1)S(1)} %copy-done, bf16[4096,4096]{1,0:T(8,128)(2,1)} %all-gather.2.cloned.1.call-done), kind=kOutput, calls=%fused_computation.17 | convolution fusion | flops 8590983168 | bytes 39846912 | tf_op jit(solution)/shard_map/dot_general | solution.py:11
  313.0 0.0 copy-start.4
  313.0 10.2 %pmax.7 = f32[256]{0:T(256)S(1)} all-reduce(f32[256]{0:T(256)S(1)} %get-tuple-element.9), channel_id=1, replica_groups=mesh['dp'=8,'vocab'=4] {'vocab'}, use_global_device_ids=true, to_apply=%region_1.2 | all-reduce | flops 256 | bytes 2048 | tf_op jit(solution)/shard_map/pmax | solution.py:17
  323.1 3.5 select_reduce_fusion
  326.6 8.0 %all-reduce.3 = (f32[256]{0:T(256)S(1)}, f32[256]{0:T(256)S(1)}) all-reduce(f32[256]{0:T(256)S(1)} %get-tuple-element.4, f32[256]{0:T(256)S(1)} %get-tuple-element.3), channel_id=1, replica_groups=mesh['dp'=8,'vocab'=4] {'vocab'}, use_global_device_ids=true, to_apply=%region_3.4 | all-reduce | flops 512 | bytes 4096 | tf_op jit(solution)/shard_map/psum | solution.py:19
  334.6 0.0 copy-done.4
  334.6 25.9 %fusion.6 = f32[4096,4096]{1,0:T(8,128)} fusion(bf16[256,4096]{1,0:T(8,128)(2,1)S(1)} %copy-done, f32[256,4096]{1,0:T(8,128)} %get-tuple-element.10, s32[256]{0:T(256)S(1)} %broadcast_subtract_fusion, f32[256]{0:T(256)S(1)} %get-tuple-element.7, f32[256]{0:T(256)S(1)} %pmax.7, f32[256]{0:T(256)S(1)} %copy-done.4), kind=kOutput, calls=%fused_computation.16 | convolution fusion | flops 8597274624 | bytes 73404416 | tf_op jit(solution)/shard_map/dot_general | solution.py:38
  360.5 34.7 %add_convert_fusion = bf16[4096,4096]{1,0:T(8,128)(2,1)} fusion(f32[4096,4096]{1,0:T(8,128)} %fusion.6, bf16[64,4096]{1,0:T(8,128)(2,1)S(1)} %all_gather.19, bf16[64,4096]{1,0:T(8,128)(2,1)S(1)} %all_gather.18, s32[128]{0:T(128)S(1)} %add_subtract_fusion.1), kind=kOutput, calls=%fused_computation | convolution fusion | flops 4331143168 | bytes 101712384 | tf_op jit(solution)/shard_map/dot_general | solution.py:37
  395.2 0.0 reduce-scatter.5.cloned.1.call-update
  395.2 0.2 reduce-scatter.3.cloned.1.call-start
  395.4 18.5 %convolution_convert_fusion = bf16[256,4096]{1,0:T(8,128)(2,1)} fusion(bf16[4096,4096]{1,0:T(8,128)(2,1)} %all-gather.2.cloned.1.call-done, f32[256,4096]{1,0:T(8,128)} %get-tuple-element.10, s32[256]{0:T(256)S(1)} %broadcast_subtract_fusion, f32[256]{0:T(256)S(1)} %get-tuple-element.7, f32[256]{0:T(256)S(1)} %pmax.7, f32[256]{0:T(256)S(1)} %copy-done.4), kind=kOutput, calls=%fused_computation.1 | convolution fusion | flops 8598323200 | bytes 39849984 | tf_op jit(solution)/shard_map/dot_general | solution.py:24
  414.0 0.0 reduce-scatter.3.cloned.1.call-update
  414.0 0.0 copy-start.1
  414.0 0.6 add_subtract_fusion
  414.6 303.5 %reduce-scatter.5.cloned.1.call-done = bf16[512,4096]{1,0:T(8,128)(2,1)} async-done(((bf16[4096,4096]{1,0:T(8,128)(2,1)}), bf16[512,4096]{1,0:T(8,128)(2,1)}) %reduce-scatter.5.cloned.1.call-update) | async-done | bytes 4194320 | tf_op jit(solution)/shard_map/reduce_scatter | solution.py:41
  718.1 6.7 convert_element_type.20
  724.8 33.6 %reduce-scatter.3.cloned.1.call-done = bf16[256,1024]{1,0:T(8,128)(2,1)} async-done(((bf16[256,4096]{1,0:T(8,128)(2,1)}), bf16[256,1024]{1,0:T(8,128)(2,1)}) %reduce-scatter.3.cloned.1.call-update) | async-done | bytes 524304 | tf_op jit(solution)/shard_map/reduce_scatter | solution.py:25
  758.4 0.0 copy-done.1
  (3 shorter events, 0.0 us)
Async XLA Ops:
  7.2 289.4 %copy-start = (bf16[256,4096]{1,0:T(8,128)(2,1)S(1)}, bf16[256,4096]{1,0:T(8,128)(2,1)}, u32[]{:S(2)}) copy-start(bf16[256,4096]{1,0:T(8,128)(2,1)} %param.8) | copy-start | bytes 6291460
  7.2 0.9 copy-start.8
  7.2 2.1 copy-start.6
  7.2 2.3 copy-start.7
  7.2 9.9 %copy-start.2 = (bf16[16,4096]{1,0:T(8,128)(2,1)S(1)}, bf16[16,4096]{1,0:T(8,128)(2,1)}, u32[]{:S(2)}) copy-start(bf16[16,4096]{1,0:T(8,128)(2,1)} %param.13) | copy-start | bytes 393220
  7.2 20.3 %copy-start.3 = (bf16[16,4096]{1,0:T(8,128)(2,1)S(1)}, bf16[16,4096]{1,0:T(8,128)(2,1)}, u32[]{:S(2)}) copy-start(bf16[16,4096]{1,0:T(8,128)(2,1)} %param.15) | copy-start | bytes 393220
  7.2 29.9 %copy-start.5 = (s32[256]{0:T(256)S(1)}, s32[256]{0:T(256)}, u32[]{:S(2)}) copy-start(s32[256]{0:T(256)} %param.10) | copy-start | bytes 3076
  7.2 289.3 %all-gather.2.cloned.1.call-start = ((), (), s32[]{:S(2)}) async-start(), calls=%async_computation.2 | async-start | bytes 37748736 | tf_op jit(solution)/shard_map/all_gather | solution.py:10
  8.0 710.1 %reduce-scatter.5.cloned.1.call-start = ((), (), s32[]{:S(2)}) async-start(), calls=%async_computation.4 | async-start | bytes 37748736 | tf_op jit(solution)/shard_map/reduce_scatter | solution.py:41
  313.0 21.6 %copy-start.4 = (f32[256]{0:T(256)S(1)}, f32[256]{0:T(256)}, u32[]{:S(2)}) copy-start(f32[256]{0:T(256)} %param.11) | copy-start | bytes 3076
  395.2 363.2 %reduce-scatter.3.cloned.1.call-start = ((), (), s32[]{:S(2)}) async-start(), calls=%async_computation.3 | async-start | bytes 2621440 | tf_op jit(solution)/shard_map/reduce_scatter | solution.py:25
  414.0 344.4 %copy-start.1 = (bf16[256,4096]{1,0:T(8,128)(2,1)S(1)}, bf16[256,4096]{1,0:T(8,128)(2,1)}, u32[]{:S(2)}) copy-start(bf16[256,4096]{1,0:T(8,128)(2,1)} %param.8) | copy-start | bytes 6291460
Sparse Core Ops, SparseCore 0:
  9.7 286.7 all-gather.1
  395.3 322.7 reduce-scatter.4
  721.9 36.4 reduce-scatter.2
where the time goes:
time: 767 us; the launch traced here: 765 us
  waiting for transfers between devices  597 us (78%)
  matrix products  95.5 us (12%)
  blocking collectives  45.5 us (6%)
  between operations  14.5 us (2%)
  other arithmetic  10.8 us (1%)
    reduce_scatter x1, waiting for transfers between devices, shards(): lax.psum_scatter((head + looked_up).astype(jnp.bfloat16), 'dp', scatter_d...  304 us
    all_gather x1, waiting for transfers between devices, shards(): gathered = lax.all_gather(table, 'dp', axis=0, tiled=True)  259 us
    dot_general x1, matrix products, shards(): looked_up = jnp.dot(hits, all_cot, preferred_element_type=jnp.float32)  34.7 us
    reduce_scatter x1, waiting for transfers between devices, shards(): lax.psum_scatter(state_term.astype(jnp.bfloat16), 'vocab', scatter_dimens...  33.6 us
    dot_general x1, matrix products, shards(): lax.dot_general(dlogits, hidden, (((0,), (0,)), ((), ())), preferred_elem...  25.9 us
    dot_general x1, matrix products, shards(): state_term = jnp.dot(dlogits, gathered, preferred_element_type=jnp.float32)  18.5 us
    dot_general x1, matrix products, shards(): logits = jnp.dot(hidden, gathered.T, preferred_element_type=jnp.float32)  16.4 us
  transfers between devices with their start and end apart: 3, of which 3 were waited for; matrix products, arithmetic and copies ran while one was open for 4% of the time, Pallas kernels for 0%

commit v1 on v0

v1 whole, which is shorter than its diff:
```python
import jax
import jax.numpy as jnp
from jax import lax
from jax.sharding import PartitionSpec as P

F32 = jnp.float32
BOTH = ("dp", "vocab")


def dot(a, b, dims):
    return lax.dot_general(a, b, (dims, ((), ())), preferred_element_type=F32)


def shards(hidden, table, targets, token_scale, enc_ids, enc_cot, dec_ids, dec_cot):
    n_dp, n_vocab = lax.axis_size("dp"), lax.axis_size("vocab")
    me_dp, me_vocab = lax.axis_index("dp"), lax.axis_index("vocab")
    tok, width = hidden.shape
    rows = table.shape[0]
    cols = width // n_vocab
    tokens = tok * n_dp
    offset = (me_vocab * n_dp + me_dp) * rows

    mine = lax.dynamic_slice_in_dim(hidden, me_vocab * cols, cols, 1)
    states = lax.all_gather(mine, BOTH, axis=0).reshape(n_dp, n_vocab, tok, cols)
    states = [states[:, v].reshape(tokens, cols) for v in range(n_vocab)]
    parts = [table[:, v * cols:(v + 1) * cols] for v in range(n_vocab)]

    small = lax.all_gather(
        jnp.stack([targets.astype(F32), token_scale]), "dp", axis=0
    )
    all_targets = small[:, 0].reshape(tokens).astype(jnp.int32) - offset
    all_scale = small[:, 1].reshape(tokens)

    logits = sum(dot(h, t, ((1,), (1,))) for h, t in zip(states, parts))
    columns = jnp.arange(rows, dtype=jnp.int32)
    matches = columns[None, :] == all_targets[:, None]
    target_part = jnp.sum(jnp.where(matches, logits, 0.0), axis=1)
    local_max = jnp.max(logits, axis=1)
    local_sum = jnp.sum(jnp.exp(logits - local_max[:, None]), axis=1)
    stats = lax.all_gather(jnp.stack([local_max, local_sum, target_part]), BOTH, axis=0)
    row_max = jnp.max(stats[:, 0], axis=0)
    row_sum = jnp.sum(stats[:, 1] * jnp.exp(stats[:, 0] - row_max[None]), axis=0)
    target_logit = jnp.sum(stats[:, 2], axis=0)
    loss = row_max + jnp.log(row_sum) - target_logit
    loss = lax.dynamic_slice_in_dim(loss, me_dp * tok, tok, 0)

    dlogits = (
        all_scale[:, None]
        * (jnp.exp(logits - row_max[:, None]) / row_sum[:, None] - matches.astype(F32))
    ).astype(jnp.bfloat16)

    everyone = n_dp * n_vocab
    steps = 1 if tokens * width * 2 <= (16 << 20) else 4
    short = tok // steps
    by_group = dlogits.reshape(n_dp, tok, rows)
    done = []
    for step in range(steps):
        part = by_group[:, step * short:(step + 1) * short].reshape(n_dp * short, rows)
        if done:
            part, done[-1] = lax.optimization_barrier((part, done[-1]))
        terms = [
            dot(part, t, ((1,), (0,))).astype(jnp.bfloat16).reshape(n_dp, short, cols)
            for t in parts
        ]
        terms = jnp.stack(terms, axis=1).reshape(everyone, short, cols)
        done.append(lax.psum_scatter(terms, BOTH, scatter_dimension=0, tiled=False))
    grad_hidden = jnp.concatenate(done, axis=0)

    head = jnp.concatenate([dot(dlogits, h, ((0,), (0,))) for h in states], axis=1)

    ids = jnp.concatenate([enc_ids, dec_ids])
    cots = jnp.concatenate([enc_cot, dec_cot], axis=0)
    per = ids.shape[0]
    pieces = max(1, everyone * per * width * 2 // (8 << 20))
    all_ids = lax.all_gather(ids.reshape(pieces, per // pieces), BOTH, axis=1, tiled=True)

    def add(total, piece):
        one_ids, one_cots = piece
        got = lax.all_gather(one_cots, BOTH, axis=0, tiled=True)
        hits = (columns[:, None] == (one_ids - offset)[None, :]).astype(jnp.bfloat16)
        return total + dot(hits, got, ((1,), (0,))), None

    cots = cots.reshape(pieces, per // pieces, width)
    if pieces == 1:
        grad_table, _ = add(head, (all_ids[0], cots[0]))
    else:
        grad_hidden, head = lax.optimization_barrier((grad_hidden, head))
        grad_table, _ = lax.scan(add, head, (all_ids, cots))
    return (grad_hidden, grad_table, loss)


def solution(mesh):
    placed = (
        P("dp", None),
        P(("vocab", "dp"), None),
        P("dp"),
        P("dp"),
        P(("dp", "vocab")),
        P(("dp", "vocab"), None),
        P(("dp", "vocab")),
        P(("dp", "vocab"), None),
    )
    return jax.shard_map(
        shards,
        mesh=mesh,
        in_specs=placed,
        out_specs=(P("dp", "vocab"), P(("vocab", "dp"), None), P("dp")),
        check_vma=False,
    )
```

time: 767 us -> 609 us (0.79)
  waiting for transfers between devices: 597 us -> 385 us
  blocking collectives: 45.5 us -> 131 us
  matrix products: 95.5 us -> 50.4 us
  local copies, waits for them, and re-layouts: 1.1 us -> 18.4 us
    all_gather x1 -> x2, waiting for transfers between devices: 259 us -> 101 us  [the longest x1 101 us: shards(): lax.all_gather(mine, BOTH, axis=0).reshape(n_dp, n_vocab, tok, cols)]
    all_gather x2, blocking collectives: 19.9 us -> 83.4 us  [the longest x1 70.4 us: shards(): lax.all_gather(jnp.stack([local_max, local_sum, target_part]), BOTH, axis=0)]
    reduce_scatter x2 -> x1, waiting for transfers between devices: 337 us -> 284 us  [shards(): done.append(lax.psum_scatter(terms, BOTH, scatter_dimension=0, tiled=False))]
    dot_general x4 -> x13, matrix products: 95.5 us -> 50.4 us  [dot(): return lax.dot_general(a, b, (dims, ((), ())), preferred_element_type=F32)]
    unnamed x1, blocking collectives: 7.37 us -> 47.4 us
    pmax x1 -> x0, blocking collectives: 10.2 us -> none  [shards(): row_max = lax.pmax(local_max, 'vocab')]
    psum x1 -> x0, blocking collectives: 7.98 us -> none  [shards(): lax.psum((jnp.sum(expo, axis=1), target_part), 'vocab')]
  transfers between devices with their start and end apart: 3 -> 3, of which waited for: 3 -> 2; matrix products, arithmetic and copies ran while one was open for 4% -> 12% of each run, Pallas kernels for 0% -> 0%
where the time goes in v1:
time: 609 us; the launch traced here: 608 us
  waiting for transfers between devices  385 us (63%)
  blocking collectives  131 us (22%)
  matrix products  50.4 us (8%)
  local copies, waits for them, and re-layouts  18.4 us (3%)
  between operations  14 us (2%)
  other arithmetic  9.32 us (2%)
    reduce_scatter x1, waiting for transfers between devices, shards(): done.append(lax.psum_scatter(terms, BOTH, scatter_dimension=0, tiled=False))  284 us
    all_gather x1, waiting for transfers between devices, shards(): lax.all_gather(mine, BOTH, axis=0).reshape(n_dp, n_vocab, tok, cols)  101 us
    all_gather x1, blocking collectives, shards(): lax.all_gather(jnp.stack([local_max, local_sum, target_part]), BOTH, axis=0)  70.4 us
    dot_general x13, matrix products, dot(): return lax.dot_general(a, b, (dims, ((), ())), preferred_element_type=F32)  50.4 us
    unnamed x1, blocking collectives  47.4 us
    all_gather x1, blocking collectives, shards(): lax.all_gather(jnp.stack([targets.astype(F32), token_scale]), 'dp', axis=0)  12.9 us
  transfers between devices with their start and end apart: 3, of which 2 were waited for; matrix products, arithmetic and copies ran while one was open for 12% of the time, Pallas kernels for 0%

profile of v1, /device:TPU:8, one launch (start us, length us, event | category | flops | bytes accessed | tf_op | source)
XLA Modules:
  0.0 607.7 jit_solution(11568275393556344522)
XLA Ops:
  7.2 0.0 copy-start
  7.2 0.0 all-gather.11.cloned.1.call-start
  7.2 1.5 copy-done
  8.8 0.8 constant_dynamic-slice_fusion
  9.6 0.0 all-gather.11.cloned.1.call-update
  9.6 0.0 all-gather.9.cloned.1.call-start
  9.7 1.7 pad_maximum_fusion.1
  11.4 0.0 all-gather.9.cloned.1.call-update
  11.4 0.0 reduce-scatter.2.cloned.1.call-start
  11.4 0.7 convert_element_type.30
  12.1 0.7 maximum_bitcast_fusion.1
  12.8 12.9 %all-gather.4 = f32[8,2,256]{2,1,0:T(2,128)S(1)} all-gather(f32[1,2,256]{2,1,0:T(2,128)S(1)} %maximum_bitcast_fusion.1), channel_id=2, replica_groups=mesh['dp'=8,'vocab'=4] {'dp'}, dimensions={0}, use_global_device_ids=true | all-gather | bytes 18432 | tf_op jit(solution)/shard_map/all_gather | solution.py:28
  25.8 100.7 %all-gather.11.cloned.1.call-done = bf16[8192,1024]{1,0:T(8,128)(2,1)} async-done(((bf16[256,1024]{1,0:T(8,128)(2,1)}), bf16[8192,1024]{1,0:T(8,128)(2,1)}) %all-gather.11.cloned.1.call-update) | async-done | bytes 16777232 | tf_op jit(solution)/shard_map/all_gather | solution.py:24
  126.4 6.9 %fusion.17 = (bf16[8,1,256,1024]{3,2,1,0:T(8,128)(2,1)S(1)}, bf16[8,1,256,1024]{3,2,1,0:T(8,128)(2,1)S(1)}, bf16[8,1,256,1024]{3,2,1,0:T(8,128)(2,1)S(1)}, bf16[8,1,256,1024]{3,2,1,0:T(8,128)(2,1)S(1)}) fusion(bf16[8,4,256,1024]{3,2,1,0:T(8,128)(2,1)} %bitcast.54), kind=kLoop, calls=%fused_computation.42 | loop fusion | bytes 33554432 | tf_op jit(solution)/shard_map/slice | solution.py:25
  133.3 0.0 copy-start.4
  133.3 0.0 copy-start.8
  133.3 0.0 copy-start.6
  133.3 0.0 copy-start.2
  133.3 0.0 copy-start.9
  133.4 4.6 fusion.10
  137.9 0.0 copy-done.4
  137.9 1.7 copy-done.9
  139.7 2.4 fusion.4
  142.1 0.0 copy-done.8
  142.1 0.0 copy-done.6
  142.1 0.0 copy-start.10
  142.1 2.4 fusion.7
  144.5 0.0 copy-done.2
  144.5 0.0 copy-done.10
  144.5 2.6 fusion.18
  147.1 1.1 exponential_reduce_fusion
  148.3 70.4 %all-gather.5 = f32[32,3,2048]{2,1,0:T(4,128)S(1)} all-gather(f32[1,3,2048]{2,1,0:T(4,128)S(1)} %maximum_bitcast_fusion), channel_id=4, replica_groups=mesh['dp'=8,'vocab'=4] {'dp','vocab'}, dimensions={0}, use_global_device_ids=true | all-gather | bytes 811008 | tf_op jit(solution)/shard_map/all_gather | solution.py:40
  218.7 0.6 slice_reduce_fusion
  219.4 0.2 fusion.15
  219.5 1.3 multiply_convert_fusion
  220.9 2.4 convolution_convert_fusion.3
  223.2 2.4 convolution_convert_fusion.2
  225.6 2.4 convolution_convert_fusion.1
  228.0 2.4 convolution_convert_fusion
  230.4 2.2 pad_maximum_fusion
  232.7 6.7 %copy.14 = bf16[8,4,256,1024]{3,2,1,0:T(8,128)(2,1)} copy(bf16[8,4,256,1024]{3,2,0,1:T(8,128)(2,1)S(1)} %pad_maximum_fusion) | data formatting | bytes 33554432 | tf_op jit(solution)/shard_map/stack | solution.py:65
  239.3 0.0 copy-start.11
  239.3 0.0 copy-start.12
  239.3 0.0 reduce-scatter.2.cloned.1.call-update
  239.4 0.6 copy-done.11
  240.0 0.0 copy-done.12
  240.0 0.2 add_dynamic-update-slice_fusion
  240.2 47.4 %all-reduce = s32[1024]{0:T(1024)S(1)} all-reduce(s32[1024]{0:T(1024)S(1)} %add_dynamic-update-slice_fusion), channel_id=5, replica_groups=mesh['dp'=8,'vocab'=4] {'dp','vocab'}, use_global_device_ids=true, to_apply=%add | all-reduce | flops 1024 | bytes 8192
  287.6 0.6 dynamic-slice_subtract_fusion
  288.2 0.0 copy-start.7
  288.2 6.0 fusion.19
  294.3 0.0 copy-done.7
  294.3 0.0 copy-start.5
  294.3 3.7 fusion.20
  298.0 0.0 copy-done.5
  298.0 0.0 copy-start.3
  298.0 3.7 fusion.21
  301.7 0.0 copy-done.3
  301.7 3.7 fusion.22
  305.4 0.0 all-gather.9.cloned.1.call-done
  305.4 0.0 copy-start.1
  305.4 11.7 %maximum_add_fusion = f32[512,4096]{1,0:T(8,128)} fusion(f32[512,1024]{1,0:T(8,128)} %fusion.22, f32[512,1024]{1,0:T(8,128)} %fusion.21, f32[512,1024]{1,0:T(8,128)} %fusion.20, f32[512,1024]{1,0:T(8,128)} %fusion.19, bf16[1024,4096]{1,0:T(8,128)(2,1)} %all-gather.9.cloned.1.call-done, s32[1024]{0:T(1024)S(1)} %broadcast_subtract_fusion), kind=kOutput, calls=%fused_computation.1 | convolution fusion | flops 4303880192 | bytes 25169920 | tf_op jit(solution)/shard_map/dot_general | solution.py:11
  317.1 284.0 %reduce-scatter.2.cloned.1.call-done = bf16[1,256,1024]{2,1,0:T(8,128)(2,1)} async-done(((bf16[32,256,1024]{2,1,0:T(8,128)(2,1)}), bf16[1,256,1024]{2,1,0:T(8,128)(2,1)}) %reduce-scatter.2.cloned.1.call-update) | async-done | bytes 524304 | tf_op jit(solution)/shard_map/reduce_scatter | solution.py:66
  601.1 0.0 copy-done.1
  (5 shorter events, 0.1 us)
Async XLA Ops:
  7.2 1.6 copy-start
  7.2 119.3 %all-gather.11.cloned.1.call-start = ((), (), s32[]{:S(2)}) async-start(), calls=%async_computation.3 | async-start | bytes 17301504 | tf_op jit(solution)/shard_map/all_gather | solution.py:24
  9.6 295.8 %all-gather.9.cloned.1.call-start = ((), (), s32[]{:S(2)}) async-start(), calls=%async_computation.2 | async-start | bytes 8650752 | tf_op jit(solution)/shard_map/all_gather | solution.py:79
  11.4 589.8 %reduce-scatter.2.cloned.1.call-start = ((), (), s32[]{:S(2)}) async-start(), calls=%async_computation.1 | async-start | bytes 17301504 | tf_op jit(solution)/shard_map/reduce_scatter | solution.py:66
  133.3 4.6 copy-start.4
  133.3 8.7 %copy-start.8 = (bf16[8,1,256,1024]{3,2,1,0:T(8,128)(2,1)}, bf16[8,1,256,1024]{3,2,1,0:T(8,128)(2,1)S(1)}, u32[]{:S(2)}) copy-start(bf16[8,1,256,1024]{3,2,1,0:T(8,128)(2,1)S(1)} %get-tuple-element.10) | copy-start | bytes 12582916
  133.3 8.7 %copy-start.6 = (bf16[8,1,256,1024]{3,2,1,0:T(8,128)(2,1)}, bf16[8,1,256,1024]{3,2,1,0:T(8,128)(2,1)S(1)}, u32[]{:S(2)}) copy-start(bf16[8,1,256,1024]{3,2,1,0:T(8,128)(2,1)S(1)} %get-tuple-element.9) | copy-start | bytes 12582916
  133.3 11.1 %copy-start.2 = (bf16[8,1,256,1024]{3,2,1,0:T(8,128)(2,1)}, bf16[8,1,256,1024]{3,2,1,0:T(8,128)(2,1)S(1)}, u32[]{:S(2)}) copy-start(bf16[8,1,256,1024]{3,2,1,0:T(8,128)(2,1)S(1)} %get-tuple-element.7) | copy-start | bytes 12582916
  133.3 6.3 %copy-start.9 = (bf16[512,4096]{1,0:T(8,128)(2,1)S(1)}, bf16[512,4096]{1,0:T(8,128)(2,1)}, u32[]{:S(2)}) copy-start(bf16[512,4096]{1,0:T(8,128)(2,1)} %param.9) | copy-start | bytes 12582916
  142.1 2.4 copy-start.10
  239.3 0.7 copy-start.11
  239.3 0.7 copy-start.12
  288.2 6.0 copy-start.7
  294.3 3.7 copy-start.5
  298.0 3.7 copy-start.3
  305.4 295.7 %copy-start.1 = (bf16[256,4096]{1,0:T(8,128)(2,1)S(1)}, bf16[256,4096]{1,0:T(8,128)(2,1)}, u32[]{:S(2)}) copy-start(bf16[256,4096]{1,0:T(8,128)(2,1)} %param.8) | copy-start | bytes 6291460
Sparse Core Ops, SparseCore 0:
  11.5 114.9 all-gather.10
  129.3 86.2 all-gather.8
  239.5 361.6 reduce-scatter.1

commit v2 on v1

--- a/solution.py
+++ b/solution.py
@@ -9,6 +9,76 @@
 
 def dot(a, b, dims):
     return lax.dot_general(a, b, (dims, ((), ())), preferred_element_type=F32)
+
+
+def plus(kept, got):
+    return (kept.astype(F32) + got.astype(F32)).astype(jnp.bfloat16)
+
+
+def scatter_by_axes(dlogits, table, tok):
+    n_dp, me_dp = lax.axis_size("dp"), lax.axis_index("dp")
+    me_vocab = lax.axis_index("vocab")
+    n_z = n_dp // 2
+    z, core, y, x = me_dp // 2, me_dp % 2, me_vocab // 2, me_vocab % 2
+    rows, width = table.shape
+    cols = width // 4
+
+    groups = dlogits.reshape(n_z, 2, tok, rows)
+
+    def term(which):
+        part = lax.dynamic_index_in_dim(groups, which, 1, keepdims=False)
+        return dot(part.reshape(n_z * tok, rows), table, ((1,), (0,)))
+
+    twin = [(i, i ^ 1) for i in range(n_dp)]
+    got = lax.ppermute(term(1 - core).astype(jnp.bfloat16), "dp", twin)
+    both = plus(term(core), got).reshape(n_z, tok, width)
+
+    along_x = [(v, v ^ 1) for v in range(4)]
+    along_y = [(v, v ^ 2) for v in range(4)]
+
+    def block(array, index, many=1):
+        return lax.dynamic_slice_in_dim(array, index * cols, many * cols, 2)
+
+    def pair(array, index):
+        return jnp.concatenate([block(array, index), block(array, 2 + index)], axis=2)
+
+    one, two = both[:, :tok // 2], both[:, tok // 2:]
+    got_one = lax.ppermute(pair(one, 1 - x), "vocab", along_x)
+    got_two = lax.ppermute(block(two, 2 * (1 - y), 2), "vocab", along_y)
+    one = plus(pair(one, x), got_one)
+    two = plus(block(two, 2 * y, 2), got_two)
+    got_one = lax.ppermute(block(one, 1 - y), "vocab", along_y)
+    got_two = lax.ppermute(block(two, 1 - x), "vocab", along_x)
+    one = plus(block(one, y), got_one)
+    two = plus(block(two, x), got_two)
+    mine = jnp.concatenate([one, two], axis=1)
+
+    total = lax.dynamic_index_in_dim(mine, z, 0, keepdims=False).astype(F32)
+    for shift in range(1, n_z):
+        sent = lax.dynamic_index_in_dim(mine, (z + shift) % n_z, 0, keepdims=False)
+        hop = [(i, (i + 2 * shift) % n_dp) for i in range(n_dp)]
+        total = total + lax.ppermute(sent, "dp", hop).astype(F32)
+    return total.astype(jnp.bfloat16)
+
+
+def scatter_whole(dlogits, parts, tok):
+    n_dp, everyone = lax.axis_size("dp"), lax.axis_size(BOTH)
+    rows, cols = parts[0].shape
+    steps = 4
+    short = tok // steps
+    by_group = dlogits.reshape(n_dp, tok, rows)
+    done = []
+    for step in range(steps):
+        part = by_group[:, step * short:(step + 1) * short].reshape(n_dp * short, rows)
+        if done:
+            part, done[-1] = lax.optimization_barrier((part, done[-1]))
+        terms = [
+            dot(part, t, ((1,), (0,))).astype(jnp.bfloat16).reshape(n_dp, short, cols)
+            for t in parts
+        ]
+        terms = jnp.stack(terms, axis=1).reshape(everyone, short, cols)
+        done.append(lax.psum_scatter(terms, BOTH, scatter_dimension=0, tiled=False))
+    return jnp.concatenate(done, axis=0)
 
 
 def shards(hidden, table, targets, token_scale, enc_ids, enc_cot, dec_ids, dec_cot):
@@ -37,7 +107,15 @@
     target_part = jnp.sum(jnp.where(matches, logits, 0.0), axis=1)
     local_max = jnp.max(logits, axis=1)
     local_sum = jnp.sum(jnp.exp(logits - local_max[:, None]), axis=1)
-    stats = lax.all_gather(jnp.stack([local_max, local_sum, target_part]), BOTH, axis=0)
+    ids = jnp.concatenate([enc_ids, dec_ids])
+    per = ids.shape[0]
+    cots = jnp.concatenate([enc_cot, dec_cot], axis=0)
+    own = jnp.concatenate([local_max, local_sum, target_part, ids.astype(F32)])
+    own = jnp.pad(own, (0, -own.shape[0] % 1024)).reshape(-1, 128)
+    stats = lax.all_gather(own, BOTH, axis=0).reshape(n_dp * n_vocab, -1)
+    stats, cots = lax.optimization_barrier((stats, cots))
+    id_rows = stats[:, 3 * tokens:3 * tokens + per].astype(jnp.int32)
+    stats = stats[:, :3 * tokens].reshape(-1, 3, tokens)
     row_max = jnp.max(stats[:, 0], axis=0)
     row_sum = jnp.sum(stats[:, 1] * jnp.exp(stats[:, 0] - row_max[None]), axis=0)
     target_logit = jnp.sum(stats[:, 2], axis=0)
@@ -50,29 +128,16 @@
     ).astype(jnp.bfloat16)
 
     everyone = n_dp * n_vocab
-    steps = 1 if tokens * width * 2 <= (16 << 20) else 4
-    short = tok // steps
-    by_group = dlogits.reshape(n_dp, tok, rows)
-    done = []
-    for step in range(steps):
-        part = by_group[:, step * short:(step + 1) * short].reshape(n_dp * short, rows)
-        if done:
-            part, done[-1] = lax.optimization_barrier((part, done[-1]))
-        terms = [
-            dot(part, t, ((1,), (0,))).astype(jnp.bfloat16).reshape(n_dp, short, cols)
-            for t in parts
-        ]
-        terms = jnp.stack(terms, axis=1).reshape(everyone, short, cols)
-        done.append(lax.psum_scatter(terms, BOTH, scatter_dimension=0, tiled=False))
-    grad_hidden = jnp.concatenate(done, axis=0)
+    if n_vocab == 4 and n_dp % 2 == 0:
+        grad_hidden = scatter_by_axes(dlogits, table, tok)
+    else:
+        grad_hidden = scatter_whole(dlogits, parts, tok)
 
     head = jnp.concatenate([dot(dlogits, h, ((0,), (0,))) for h in states], axis=1)
 
-    ids = jnp.concatenate([enc_ids, dec_ids])
-    cots = jnp.concatenate([enc_cot, dec_cot], axis=0)
-    per = ids.shape[0]
     pieces = max(1, everyone * per * width * 2 // (8 << 20))
-    all_ids = lax.all_gather(ids.reshape(pieces, per // pieces), BOTH, axis=1, tiled=True)
+    all_ids = id_rows.reshape(everyone, pieces, per // pieces)
+    all_ids = all_ids.swapaxes(0, 1).reshape(pieces, everyone * (per // pieces))
 
     def add(total, piece):
         one_ids, one_cots = piece

time: 609 us -> 429 us (0.70)
  waiting for transfers between devices: 385 us -> 223 us
  blocking collectives: 131 us -> 72.6 us
  other arithmetic: 9.32 us -> 22.8 us
  matrix products: 50.4 us -> 60 us
  starting transfers between devices: 0.12 us -> 9.15 us
  local copies, waits for them, and re-layouts: 18.4 us -> 26.3 us
    reduce_scatter x1 -> x0, waiting for transfers between devices: 284 us -> none  [shards(): done.append(lax.psum_scatter(terms, BOTH, scatter_dimension=0, tiled=False))]
    ppermute x0 -> x8, waiting for transfers between devices: none -> 123 us  [the longest x1 51.2 us: scatter_by_axes(): got_two = lax.ppermute(block(two, 2 * (1 - y), 2), 'vocab', along_y)]
    unnamed x1 -> x0, blocking collectives: 47.4 us -> none
    all_gather x1, blocking collectives: 70.4 us -> 59.7 us  [shards(): stats = lax.all_gather(own, BOTH, axis=0).reshape(n_dp * n_vocab, -1)]
    convert_element_type x0 -> x6, other arithmetic: none -> 10.1 us  [the longest x4 8.16 us: plus(): return (kept.astype(F32) + got.astype(F32)).astype(jnp.bfloat16)]
    dot_general x13 -> x11, matrix products: 50.4 us -> 60 us  [dot(): return lax.dot_general(a, b, (dims, ((), ())), preferred_element_type=F32)]
    ppermute x0 -> x8, starting transfers between devices: none -> 9.07 us  [the longest x3 7.35 us: scatter_by_axes(): total = total + lax.ppermute(sent, 'dp', hop).astype(F32)]
    dynamic_slice x0 -> x5, local copies, waits for them, and re-layouts: none -> 6.87 us  [the longest x4 6.64 us: block(): return lax.dynamic_slice_in_dim(array, index * cols, many * cols, 2)]
  transfers between devices with their start and end apart: 3 -> 10, of which waited for: 2 -> 9; matrix products, arithmetic and copies ran while one was open for 12% -> 12% of each run, Pallas kernels for 0% -> 0%
where the time goes in v2:
time: 429 us
  waiting for transfers between devices  223 us (52%)
  blocking collectives  72.6 us (17%)
  matrix products  60 us (14%)
  local copies, waits for them, and re-layouts  26.3 us (6%)
  other arithmetic  22.8 us (5%)
  between operations  14.4 us (3%)
  starting transfers between devices  9.15 us (2%)
    all_gather x1, waiting for transfers between devices, shards(): lax.all_gather(mine, BOTH, axis=0).reshape(n_dp, n_vocab, tok, cols)  100 us
    dot_general x11, matrix products, dot(): return lax.dot_general(a, b, (dims, ((), ())), preferred_element_type=F32)  60 us
    all_gather x1, blocking collectives, shards(): stats = lax.all_gather(own, BOTH, axis=0).reshape(n_dp * n_vocab, -1)  59.7 us
    ppermute x1, waiting for transfers between devices, scatter_by_axes(): got_two = lax.ppermute(block(two, 2 * (1 - y), 2), 'vocab', along_y)  51.2 us
    ppermute x3, waiting for transfers between devices, scatter_by_axes(): total = total + lax.ppermute(sent, 'dp', hop).astype(F32)  39.3 us
    ppermute x1, waiting for transfers between devices, scatter_by_axes(): got = lax.ppermute(term(1 - core).astype(jnp.bfloat16), 'dp', twin)  13.5 us
    all_gather x1, blocking collectives, shards(): lax.all_gather(jnp.stack([targets.astype(F32), token_scale]), 'dp', axis=0)  12.9 us
    ppermute x1, waiting for transfers between devices, scatter_by_axes(): got_two = lax.ppermute(block(two, 1 - x), 'vocab', along_x)  8.65 us
  transfers between devices with their start and end apart: 10, of which 9 were waited for; matrix products, arithmetic and copies ran while one was open for 12% of the time, Pallas kernels for 0%

profile of v2, /device:TPU:8, one launch (start us, length us, event | category | flops | bytes accessed | tf_op | source)
XLA Modules:
  0.0 428.7 jit_solution(14234215542773539668)
XLA Ops:
  7.2 0.0 all-gather.8.cloned.1.call-start
  7.2 1.5 copy-done
  8.8 0.8 constant_dynamic-slice_fusion.9
  9.6 0.0 all-gather.8.cloned.1.call-update
  9.6 0.0 all-gather.6.cloned.1.call-start
  9.7 0.7 convert_element_type.89
  10.4 0.7 maximum_bitcast_fusion
  11.1 12.9 %all-gather.2 = f32[8,2,256]{2,1,0:T(2,128)S(1)} all-gather(f32[1,2,256]{2,1,0:T(2,128)S(1)} %maximum_bitcast_fusion), channel_id=2, replica_groups=mesh['dp'=8,'vocab'=4] {'dp'}, dimensions={0}, use_global_device_ids=true | all-gather | bytes 18432 | tf_op jit(solution)/shard_map/all_gather | solution.py:98
  24.0 0.8 add_convert_fusion.5
  24.8 1.7 pad_maximum_fusion.1
  26.5 100.0 %all-gather.8.cloned.1.call-done = bf16[8192,1024]{1,0:T(8,128)(2,1)} async-done(((bf16[256,1024]{1,0:T(8,128)(2,1)}), bf16[8192,1024]{1,0:T(8,128)(2,1)}) %all-gather.8.cloned.1.call-update) | async-done | bytes 16777232 | tf_op jit(solution)/shard_map/all_gather | solution.py:94
  126.4 6.9 %fusion.25 = (bf16[8,1,256,1024]{3,2,1,0:T(8,128)(2,1)S(1)}, bf16[8,1,256,1024]{3,2,1,0:T(8,128)(2,1)S(1)}, bf16[8,1,256,1024]{3,2,1,0:T(8,128)(2,1)S(1)}, bf16[8,1,256,1024]{3,2,1,0:T(8,128)(2,1)S(1)}) fusion(bf16[8,4,256,1024]{3,2,1,0:T(8,128)(2,1)} %bitcast.63), kind=kLoop, calls=%fused_computation.74 | loop fusion | bytes 33554432 | tf_op jit(solution)/shard_map/slice | solution.py:95
  133.4 4.6 %fusion.5 = f32[2048,512]{1,0:T(8,128)S(1)} fusion(bf16[2048,1024]{1,0:T(8,128)(2,1)S(1)} %bitcast.66, bf16[512,4096]{1,0:T(8,128)(2,1)} %param.9), kind=kOutput, calls=%fused_computation.28 | convolution fusion | flops 2147483648 | bytes 9437184 | tf_op jit(solution)/shard_map/dot_general | solution.py:11
  138.0 1.6 copy-done.19
  139.6 2.4 fusion.7
  142.1 2.4 fusion.9
  144.5 4.6 %fusion.27 = (f32[2048]{0:T(1024)S(1)}, f32[2048,512]{1,0:T(8,128)S(1)}) fusion(bf16[2048,1024]{1,0:T(8,128)(2,1)S(1)} %bitcast.61, bf16[512,4096]{1,0:T(8,128)(2,1)} %param.9, f32[2048,512]{1,0:T(8,128)S(1)} %fusion.5, f32[2048,512]{1,0:T(8,128)S(1)} %fusion.9, f32[2048,512]{1,0:T(8,128)S(1)} %fusion.7), kind=kOutput, calls=%fused_computation.76 | convolution fusion | flops 2151675904 | bytes 22028288 | tf_op jit(solution)/shard_map/dot_general | solution.py:11
  149.1 2.0 copy-done.2
  151.1 1.6 exponential_reduce_fusion
  152.7 59.7 %all_gather.22 = f32[32,56,128]{2,1,0:T(8,128)S(1)} all-gather(f32[1,56,128]{2,1,0:T(8,128)S(1)} %fusion.23), channel_id=1, replica_groups=mesh['dp'=8,'vocab'=4] {'dp','vocab'}, dimensions={0}, use_global_device_ids=true | all-gather | bytes 946176 | tf_op jit(solution)/shard_map/all_gather | solution.py:115
  212.5 0.2 copy.29
  212.6 0.1 slice.62
  212.7 0.6 reshape.54
  213.3 0.6 slice_reduce_fusion
  213.9 0.2 fusion.22
  214.1 4.2 multiply_convert_fusion
  218.3 0.2 constant_dynamic-slice_fusion.7
  218.6 6.7 %convolution_convert_fusion = bf16[1024,4096]{1,0:T(8,128)(2,1)} fusion(bf16[1024,512]{1,0:T(8,128)(2,1)S(1)} %bitcast.76, bf16[512,4096]{1,0:T(8,128)(2,1)S(1)} %copy-done.20), kind=kOutput, calls=%fused_computation.2 | convolution fusion | flops 4299161600 | bytes 13631488 | tf_op jit(solution)/shard_map/dot_general | solution.py:11
  225.3 0.0 all-gather.6.cloned.1.call-update
  225.3 13.5 %collective-permute-done = bf16[1024,4096]{1,0:T(8,128)(2,1)} collective-permute-done((bf16[1024,4096]{1,0:T(8,128)(2,1)}, bf16[1024,4096]{1,0:T(8,128)(2,1)}, u32[]{:S(2)}, u32[]{:S(2)}) %collective-permute-start) | collective-permute-done | bytes 8388640 | tf_op jit(solution)/shard_map/ppermute | solution.py:33
  238.8 8.3 %add_convert_fusion = bf16[1024,4096]{1,0:T(8,128)(2,1)S(1)} fusion(bf16[1024,4096]{1,0:T(8,128)(2,1)} %collective-permute-done, bf16[1024,512]{1,0:T(8,128)(2,1)S(1)} %bitcast.75, bf16[512,4096]{1,0:T(8,128)(2,1)} %param.9), kind=kOutput, calls=%fused_computation | convolution fusion | flops 4307550208 | bytes 22020096 | tf_op jit(solution)/shard_map/dot_general | solution.py:11
  247.1 2.4 fusion.26
  249.5 2.0 copy-done.5
  251.5 1.6 constant_dynamic-slice_fusion.1
  253.1 3.8 constant_dynamic-slice_fusion.6
  256.8 1.5 pad_maximum_fusion
  258.3 6.0 %fusion.28 = f32[512,1024]{1,0:T(8,128)} fusion(bf16[2048,512]{1,0:T(8,128)(2,1)S(1)} %multiply_convert_fusion, bf16[2048,1024]{1,0:T(8,128)(2,1)} %bitcast.71), kind=kOutput, calls=%fused_computation.77 | convolution fusion | flops 2147483648 | bytes 8388608 | tf_op jit(solution)/shard_map/dot_general | solution.py:11
  264.3 3.7 fusion.29
  268.0 51.2 %collective-permute-done.3 = bf16[4,128,2048]{2,1,0:T(8,128)(2,1)} collective-permute-done((bf16[4,128,2048]{2,1,0:T(8,128)(2,1)}, bf16[4,128,2048]{2,1,0:T(8,128)(2,1)}, u32[]{:S(2)}, u32[]{:S(2)}) %collective-permute-start.3) | collective-permute-done | bytes 2097184 | tf_op jit(solution)/shard_map/ppermute | solution.py:47
  319.2 2.5 add_convert_fusion.1
  321.7 1.2 constant_dynamic-slice_fusion
  322.9 6.6 %collective-permute-done.1 = bf16[4,128,2048]{2,1,0:T(8,128)(2,1)} collective-permute-done((bf16[4,128,2048]{2,1,0:T(8,128)(2,1)}, bf16[4,128,2048]{2,1,0:T(8,128)(2,1)}, u32[]{:S(2)}, u32[]{:S(2)}) %collective-permute-start.1) | collective-permute-done | bytes 2097184 | tf_op jit(solution)/shard_map/ppermute | solution.py:46
  329.5 2.4 add_convert_fusion.2
  332.0 0.1 constant_dynamic-slice_fusion.2
  332.1 1.2 copy-done.11
  333.3 1.7 collective-permute-start.2
  335.0 0.7 convert_subtract_fusion
  335.7 0.1 sub.91
  335.8 0.6 dynamic-slice_subtract_fusion
  336.4 6.1 %fusion.30 = f32[512,1024]{1,0:T(8,128)} fusion(bf16[2048,512]{1,0:T(8,128)(2,1)S(1)} %multiply_convert_fusion, bf16[2048,1024]{1,0:T(8,128)(2,1)} %bitcast.67), kind=kOutput, calls=%fused_computation.79 | convolution fusion | flops 2147483648 | bytes 8388608 | tf_op jit(solution)/shard_map/dot_general | solution.py:11
  342.5 8.6 %collective-permute-done.4 = bf16[4,128,1024]{2,1,0:T(8,128)(2,1)} collective-permute-done((bf16[4,128,1024]{2,1,0:T(8,128)(2,1)}, bf16[4,128,1024]{2,1,0:T(8,128)(2,1)}, u32[]{:S(2)}, u32[]{:S(2)}) %collective-permute-start.4) | collective-permute-done | bytes 1048608 | tf_op jit(solution)/shard_map/ppermute | solution.py:51
  351.2 1.6 add_convert_fusion.3
  352.8 4.2 collective-permute-done.2
  357.0 1.6 add_convert_fusion.4
  358.6 0.1 fusion.16
  358.8 0.3 collective-permute-start.5
  359.0 7.0 %collective-permute-start.6 = (bf16[256,1024]{1,0:T(8,128)(2,1)S(1)}, bf16[256,1024]{1,0:T(8,128)(2,1)S(1)}, u32[]{:S(2)}, u32[]{:S(2)}) collective-permute-start(bf16[256,1024]{1,0:T(8,128)(2,1)S(1)} %get-tuple-element.22), channel_id=1, source_target_pairs={{0,16},{4,20},{8,24},{12,28},{16,0},{20,4},{24,8},{28,12},{1,17},{... | collective-permute-start | bytes 1572872 | tf_op jit(solution)/shard_map/ppermute | solution.py:60
  366.1 0.0 collective-permute-start.7
  366.1 3.7 fusion.31
  369.8 6.7 %collective-permute-done.5 = bf16[256,1024]{1,0:T(8,128)(2,1)S(1)} collective-permute-done((bf16[256,1024]{1,0:T(8,128)(2,1)S(1)}, bf16[256,1024]{1,0:T(8,128)(2,1)S(1)}, u32[]{:S(2)}, u32[]{:S(2)}) %collective-permute-start.5) | collective-permute-done | bytes 524320 | tf_op jit(solution)/shard_map/ppermute | solution.py:60
  376.6 25.2 %collective-permute-done.6 = bf16[256,1024]{1,0:T(8,128)(2,1)S(1)} collective-permute-done((bf16[256,1024]{1,0:T(8,128)(2,1)S(1)}, bf16[256,1024]{1,0:T(8,128)(2,1)S(1)}, u32[]{:S(2)}, u32[]{:S(2)}) %collective-permute-start.6) | collective-permute-done | bytes 524320 | tf_op jit(solution)/shard_map/ppermute | solution.py:60
  401.8 7.4 %collective-permute-done.7 = bf16[256,1024]{1,0:T(8,128)(2,1)S(1)} collective-permute-done((bf16[256,1024]{1,0:T(8,128)(2,1)S(1)}, bf16[256,1024]{1,0:T(8,128)(2,1)S(1)}, u32[]{:S(2)}, u32[]{:S(2)}) %collective-permute-start.7) | collective-permute-done | bytes 524320 | tf_op jit(solution)/shard_map/ppermute | solution.py:60
  409.1 1.2 fusion.2
  410.3 11.6 %maximum_add_fusion = f32[512,4096]{1,0:T(8,128)} fusion(f32[512,1024]{1,0:T(8,128)} %fusion.31, f32[512,1024]{1,0:T(8,128)} %fusion.30, f32[512,1024]{1,0:T(8,128)} %fusion.29, f32[512,1024]{1,0:T(8,128)} %fusion.28, bf16[1024,4096]{1,0:T(8,128)(2,1)} %all-gather.6.cloned.1.call-done, s32[1024]{0:T(1024)S(1)} %sub.91), kind=kOutput, calls=%fused_computation.1 | convolution fusion | flops 4303880192 | bytes 25169920 | tf_op jit(solution)/shard_map/dot_general | solution.py:11
  (45 shorter events, 0.1 us)
Async XLA Ops:
  7.2 1.6 copy-start
  7.2 119.3 %all-gather.8.cloned.1.call-start = ((), (), s32[]{:S(2)}) async-start(), calls=%async_computation.1 | async-start | bytes 17301504 | tf_op jit(solution)/shard_map/all_gather | solution.py:94
  9.6 400.6 %all-gather.6.cloned.1.call-start = ((), (), s32[]{:S(2)}) async-start(), calls=%async_computation | async-start | bytes 8650752 | tf_op jit(solution)/shard_map/all_gather | solution.py:144
  133.3 4.7 %copy-start.14 = (bf16[8,1,256,1024]{3,2,1,0:T(8,128)(2,1)}, bf16[8,1,256,1024]{3,2,1,0:T(8,128)(2,1)S(1)}, u32[]{:S(2)}) copy-start(bf16[8,1,256,1024]{3,2,1,0:T(8,128)(2,1)S(1)} %get-tuple-element.12) | copy-start | bytes 12582916
  133.3 4.7 %copy-start.15 = (bf16[8,1,256,1024]{3,2,1,0:T(8,128)(2,1)}, bf16[8,1,256,1024]{3,2,1,0:T(8,128)(2,1)S(1)}, u32[]{:S(2)}) copy-start(bf16[8,1,256,1024]{3,2,1,0:T(8,128)(2,1)S(1)} %get-tuple-element.13) | copy-start | bytes 12582916
  133.3 8.7 %copy-start.17 = (bf16[8,1,256,1024]{3,2,1,0:T(8,128)(2,1)}, bf16[8,1,256,1024]{3,2,1,0:T(8,128)(2,1)S(1)}, u32[]{:S(2)}) copy-start(bf16[8,1,256,1024]{3,2,1,0:T(8,128)(2,1)S(1)} %get-tuple-element.14) | copy-start | bytes 12582916
  133.3 11.1 %copy-start.3 = (bf16[8,1,256,1024]{3,2,1,0:T(8,128)(2,1)}, bf16[8,1,256,1024]{3,2,1,0:T(8,128)(2,1)S(1)}, u32[]{:S(2)}) copy-start(bf16[8,1,256,1024]{3,2,1,0:T(8,128)(2,1)S(1)} %get-tuple-element.11) | copy-start | bytes 12582916
  133.3 6.3 %copy-start.19 = (bf16[512,4096]{1,0:T(8,128)(2,1)S(1)}, bf16[512,4096]{1,0:T(8,128)(2,1)}, u32[]{:S(2)}) copy-start(bf16[512,4096]{1,0:T(8,128)(2,1)} %param.9) | copy-start | bytes 12582916
  149.1 2.0 copy-start.2
  212.6 1.5 copy-start.18
  214.1 4.4 %copy-start.20 = (bf16[512,4096]{1,0:T(8,128)(2,1)S(1)}, bf16[512,4096]{1,0:T(8,128)(2,1)}, u32[]{:S(2)}) copy-start(bf16[512,4096]{1,0:T(8,128)(2,1)} %param.9) | copy-start | bytes 12582916
  218.3 118.1 %copy-start.7 = (bf16[2048,512]{1,0:T(8,128)(2,1)}, bf16[2048,512]{1,0:T(8,128)(2,1)S(1)}, u32[]{:S(2)}) copy-start(bf16[2048,512]{1,0:T(8,128)(2,1)S(1)} %multiply_convert_fusion) | copy-start | bytes 6291460
  225.3 13.5 %collective-permute-start = (bf16[1024,4096]{1,0:T(8,128)(2,1)}, bf16[1024,4096]{1,0:T(8,128)(2,1)}, u32[]{:S(2)}, u32[]{:S(2)}) collective-permute-start(bf16[1024,4096]{1,0:T(8,128)(2,1)} %convolution_convert_fusion), channel_id=1, source_target_pairs={{0,4},{4,0},{8,12},{12,8},{16,20},{20,16},{24,28},{28,24},{1,5},{5... | collective-permute-start | bytes 25165832 | tf_op jit(solution)/shard_map/ppermute | solution.py:33
  249.5 2.0 copy-start.5
  253.1 66.2 %collective-permute-start.3 = (bf16[4,128,2048]{2,1,0:T(8,128)(2,1)}, bf16[4,128,2048]{2,1,0:T(8,128)(2,1)}, u32[]{:S(2)}, u32[]{:S(2)}) collective-permute-start(bf16[4,128,2048]{2,1,0:T(8,128)(2,1)} %constant_dynamic-slice_fusion.1), channel_id=1, source_target_pairs={{0,2},{1,3},{2,0},{3,1},{4,6},{5,7},{6,4},{7,5},{8,10},{9,11},{10,... | collective-permute-start | bytes 6291464 | tf_op jit(solution)/shard_map/ppermute | solution.py:47
  258.3 71.2 %collective-permute-start.1 = (bf16[4,128,2048]{2,1,0:T(8,128)(2,1)}, bf16[4,128,2048]{2,1,0:T(8,128)(2,1)}, u32[]{:S(2)}, u32[]{:S(2)}) collective-permute-start(bf16[4,128,2048]{2,1,0:T(8,128)(2,1)} %pad_maximum_fusion), channel_id=1, source_target_pairs={{0,1},{1,0},{2,3},{3,2},{4,5},{5,4},{6,7},{7,6},{8,9},{9,8},{10,11... | collective-permute-start | bytes 6291464 | tf_op jit(solution)/shard_map/ppermute | solution.py:46
  258.3 6.0 %copy-start.16 = (bf16[8,1,256,1024]{3,2,1,0:T(8,128)(2,1)S(1)}, bf16[8,1,256,1024]{3,2,1,0:T(8,128)(2,1)}, u32[]{:S(2)}) copy-start(bf16[8,1,256,1024]{3,2,1,0:T(8,128)(2,1)} %copy-done.15) | copy-start | bytes 12582916
  264.3 54.9 %copy-start.6 = (bf16[4,128,4096]{2,1,0:T(8,128)(2,1)S(1)}, bf16[4,128,4096]{2,1,0:T(8,128)(2,1)}, u32[]{:S(2)}) copy-start(bf16[4,128,4096]{2,1,0:T(8,128)(2,1)} %copy-done.5) | copy-start | bytes 12582916
  268.0 61.5 %copy-start.13 = (bf16[4,128,1024]{2,1,0:T(8,128)(2,1)S(1)}, bf16[4,128,1024]{2,1,0:T(8,128)(2,1)}, u32[]{:S(2)}) copy-start(bf16[4,128,1024]{2,1,0:T(8,128)(2,1)} %get-tuple-element.20) | copy-start | bytes 3145732
  321.7 10.2 %copy-start.9 = (bf16[4,128,2048]{2,1,0:T(8,128)(2,1)}, bf16[4,128,2048]{2,1,0:T(8,128)(2,1)S(1)}, u32[]{:S(2)}) copy-start(bf16[4,128,2048]{2,1,0:T(8,128)(2,1)S(1)} %add_convert_fusion.1) | copy-start | bytes 6291460
  322.9 28.3 %collective-permute-start.4 = (bf16[4,128,1024]{2,1,0:T(8,128)(2,1)}, bf16[4,128,1024]{2,1,0:T(8,128)(2,1)}, u32[]{:S(2)}, u32[]{:S(2)}) collective-permute-start(bf16[4,128,1024]{2,1,0:T(8,128)(2,1)} %constant_dynamic-slice_fusion), channel_id=1, source_target_pairs={{0,1},{1,0},{2,3},{3,2},{4,5},{5,4},{6,7},{7,6},{8,9},{9,8},{10,11... | collective-permute-start | bytes 3145736 | tf_op jit(solution)/shard_map/ppermute | solution.py:51
  332.0 1.3 copy-start.11
  333.3 23.7 %collective-permute-start.2 = (bf16[4,128,1024]{2,1,0:T(8,128)(2,1)S(1)}, bf16[4,128,1024]{2,1,0:T(8,128)(2,1)}, u32[]{:S(2)}, u32[]{:S(2)}) collective-permute-start(bf16[4,128,1024]{2,1,0:T(8,128)(2,1)S(1)} %constant_dynamic-slice_fusion.2), channel_id=1, source_target_pairs={{0,2},{1,3},{2,0},{3,1},{4,6},{5,7},{6,4},{7,5},{8,10},{9,11},{10,... | collective-permute-start | bytes 3145736 | tf_op jit(solution)/shard_map/ppermute | solution.py:50
  336.4 14.7 %copy-start.10 = (bf16[4,128,2048]{2,1,0:T(8,128)(2,1)S(1)}, bf16[4,128,2048]{2,1,0:T(8,128)(2,1)}, u32[]{:S(2)}) copy-start(bf16[4,128,2048]{2,1,0:T(8,128)(2,1)} %copy-done.9) | copy-start | bytes 6291460
  336.4 20.6 %copy-start.12 = (bf16[4,128,2048]{2,1,0:T(8,128)(2,1)S(1)}, bf16[4,128,2048]{2,1,0:T(8,128)(2,1)}, u32[]{:S(2)}) copy-start(bf16[4,128,2048]{2,1,0:T(8,128)(2,1)} %copy-done.11) | copy-start | bytes 6291460
  352.8 13.3 %copy-start.4 = (bf16[8,1,256,1024]{3,2,1,0:T(8,128)(2,1)S(1)}, bf16[8,1,256,1024]{3,2,1,0:T(8,128)(2,1)}, u32[]{:S(2)}) copy-start(bf16[8,1,256,1024]{3,2,1,0:T(8,128)(2,1)} %copy-done.3) | copy-start | bytes 12582916
  352.8 13.3 %copy-start.8 = (bf16[2048,512]{1,0:T(8,128)(2,1)S(1)}, bf16[2048,512]{1,0:T(8,128)(2,1)}, u32[]{:S(2)}) copy-start(bf16[2048,512]{1,0:T(8,128)(2,1)} %copy-done.7) | copy-start | bytes 6291460
  358.8 17.8 %collective-permute-start.5 = (bf16[256,1024]{1,0:T(8,128)(2,1)S(1)}, bf16[256,1024]{1,0:T(8,128)(2,1)S(1)}, u32[]{:S(2)}, u32[]{:S(2)}) collective-permute-start(bf16[256,1024]{1,0:T(8,128)(2,1)S(1)} %get-tuple-element.21), channel_id=1, source_target_pairs={{0,8},{4,12},{8,16},{12,20},{16,24},{20,28},{24,0},{28,4},{1,9},{5... | collective-permute-start | bytes 1572872 | tf_op jit(solution)/shard_map/ppermute | solution.py:60
  359.0 42.7 %collective-permute-start.6 = (bf16[256,1024]{1,0:T(8,128)(2,1)S(1)}, bf16[256,1024]{1,0:T(8,128)(2,1)S(1)}, u32[]{:S(2)}, u32[]{:S(2)}) collective-permute-start(bf16[256,1024]{1,0:T(8,128)(2,1)S(1)} %get-tuple-element.22), channel_id=1, source_target_pairs={{0,16},{4,20},{8,24},{12,28},{16,0},{20,4},{24,8},{28,12},{1,17},{... | collective-permute-start | bytes 1572872 | tf_op jit(solution)/shard_map/ppermute | solution.py:60
  366.1 43.0 %collective-permute-start.7 = (bf16[256,1024]{1,0:T(8,128)(2,1)S(1)}, bf16[256,1024]{1,0:T(8,128)(2,1)S(1)}, u32[]{:S(2)}, u32[]{:S(2)}) collective-permute-start(bf16[256,1024]{1,0:T(8,128)(2,1)S(1)} %get-tuple-element.23), channel_id=1, source_target_pairs={{0,24},{4,28},{8,0},{12,4},{16,8},{20,12},{24,16},{28,20},{1,25},{... | collective-permute-start | bytes 1572872 | tf_op jit(solution)/shard_map/ppermute | solution.py:60
  410.3 11.6 %copy-start.1 = (bf16[256,4096]{1,0:T(8,128)(2,1)S(1)}, bf16[256,4096]{1,0:T(8,128)(2,1)}, u32[]{:S(2)}) copy-start(bf16[256,4096]{1,0:T(8,128)(2,1)} %param.8) | copy-start | bytes 6291460
Sparse Core Ops, SparseCore 0:
  11.5 114.9 all-gather.7
  225.4 108.4 all-gather.5

commit v3 on v2

--- a/solution.py
+++ b/solution.py
@@ -110,15 +110,21 @@
     ids = jnp.concatenate([enc_ids, dec_ids])
     per = ids.shape[0]
     cots = jnp.concatenate([enc_cot, dec_cot], axis=0)
-    own = jnp.concatenate([local_max, local_sum, target_part, ids.astype(F32)])
-    own = jnp.pad(own, (0, -own.shape[0] % 1024)).reshape(-1, 128)
-    stats = lax.all_gather(own, BOTH, axis=0).reshape(n_dp * n_vocab, -1)
-    stats, cots = lax.optimization_barrier((stats, cots))
-    id_rows = stats[:, 3 * tokens:3 * tokens + per].astype(jnp.int32)
-    stats = stats[:, :3 * tokens].reshape(-1, 3, tokens)
-    row_max = jnp.max(stats[:, 0], axis=0)
-    row_sum = jnp.sum(stats[:, 1] * jnp.exp(stats[:, 0] - row_max[None]), axis=0)
-    target_logit = jnp.sum(stats[:, 2], axis=0)
+    merged = (local_max, local_sum, target_part)
+    id_rows = ids.astype(F32)[None]
+    for axis in ("vocab", "dp"):
+        own = jnp.concatenate([*merged, id_rows.reshape(-1)])
+        size = own.shape[0]
+        own = jnp.pad(own, (0, -size % 1024)).reshape(-1, 128)
+        stats = lax.all_gather(own, axis, axis=0).reshape(lax.axis_size(axis), -1)
+        id_rows = stats[:, 3 * tokens:size]
+        stats = stats[:, :3 * tokens].reshape(-1, 3, tokens)
+        row_max = jnp.max(stats[:, 0], axis=0)
+        row_sum = jnp.sum(stats[:, 1] * jnp.exp(stats[:, 0] - row_max[None]), axis=0)
+        target_logit = jnp.sum(stats[:, 2], axis=0)
+        merged = (row_max, row_sum, target_logit)
+    row_max, cots = lax.optimization_barrier((row_max, cots))
+    id_rows = id_rows.astype(jnp.int32)
     loss = row_max + jnp.log(row_sum) - target_logit
     loss = lax.dynamic_slice_in_dim(loss, me_dp * tok, tok, 0)
 

time: 429 us -> 379 us (0.88)
  blocking collectives: 72.6 us -> 34.9 us
    all_gather x1 -> x2, blocking collectives: 59.7 us -> 22 us  [shards(): stats = lax.all_gather(own, axis, axis=0).reshape(lax.axis_size(axis), -1)]
    ppermute x1, waiting for transfers between devices: 8.65 us -> 15.3 us  [scatter_by_axes(): got_two = lax.ppermute(block(two, 1 - x), 'vocab', along_x)]
    ppermute x1, waiting for transfers between devices: 6.61 us -> 0.01 us  [scatter_by_axes(): got_one = lax.ppermute(pair(one, 1 - x), 'vocab', along_x)]
    unnamed x43 -> x36, local copies, waits for them, and re-layouts: 8.62 us -> 7.3 us
  transfers between devices with their start and end apart: 10 -> 10, of which waited for: 9 -> 8; matrix products, arithmetic and copies ran while one was open for 12% -> 12% of each run, Pallas kernels for 0% -> 0%
where the time goes in v3:
time: 379 us; the launch traced here: 378 us
  waiting for transfers between devices  219 us (58%)
  matrix products  57.7 us (15%)
  blocking collectives  34.9 us (9%)
  local copies, waits for them, and re-layouts  23.3 us (6%)
  other arithmetic  19.2 us (5%)
  between operations  14.4 us (4%)
  starting transfers between devices  9.44 us (2%)
    all_gather x1, waiting for transfers between devices, shards(): lax.all_gather(mine, BOTH, axis=0).reshape(n_dp, n_vocab, tok, cols)  100 us
    dot_general x11, matrix products, dot(): return lax.dot_general(a, b, (dims, ((), ())), preferred_element_type=F32)  57.7 us
    ppermute x1, waiting for transfers between devices, scatter_by_axes(): got_two = lax.ppermute(block(two, 2 * (1 - y), 2), 'vocab', along_y)  48.2 us
    ppermute x3, waiting for transfers between devices, scatter_by_axes(): total = total + lax.ppermute(sent, 'dp', hop).astype(F32)  39.1 us
    all_gather x2, blocking collectives, shards(): stats = lax.all_gather(own, axis, axis=0).reshape(lax.axis_size(axis), -1)  22 us
    ppermute x1, waiting for transfers between devices, scatter_by_axes(): got_two = lax.ppermute(block(two, 1 - x), 'vocab', along_x)  15.3 us
    ppermute x1, waiting for transfers between devices, scatter_by_axes(): got = lax.ppermute(term(1 - core).astype(jnp.bfloat16), 'dp', twin)  13.1 us
    all_gather x1, blocking collectives, shards(): lax.all_gather(jnp.stack([targets.astype(F32), token_scale]), 'dp', axis=0)  12.9 us
  transfers between devices with their start and end apart: 10, of which 8 were waited for; matrix products, arithmetic and copies ran while one was open for 12% of the time, Pallas kernels for 0%

profile of v3, /device:TPU:8, one launch (start us, length us, event | category | flops | bytes accessed | tf_op | source)
XLA Modules:
  0.0 378.2 jit_solution(44095176859711658)
XLA Ops:
  7.2 0.0 copy-start
  7.2 0.0 all-gather.8.cloned.1.call-start
  7.2 1.5 copy-done
  8.8 0.8 constant_dynamic-slice_fusion.9
  9.6 0.0 all-gather.8.cloned.1.call-update
  9.6 0.0 all-gather.6.cloned.1.call-start
  9.7 0.7 convert_element_type.91
  10.4 0.7 maximum_bitcast_fusion
  11.1 12.9 %all-gather.2 = f32[8,2,256]{2,1,0:T(2,128)S(1)} all-gather(f32[1,2,256]{2,1,0:T(2,128)S(1)} %maximum_bitcast_fusion), channel_id=2, replica_groups=mesh['dp'=8,'vocab'=4] {'dp'}, dimensions={0}, use_global_device_ids=true | all-gather | bytes 18432 | tf_op jit(solution)/shard_map/all_gather | solution.py:98
  24.0 0.8 add_convert_fusion.5
  24.8 1.7 pad_maximum_fusion.1
  26.5 100.0 %all-gather.8.cloned.1.call-done = bf16[8192,1024]{1,0:T(8,128)(2,1)} async-done(((bf16[256,1024]{1,0:T(8,128)(2,1)}), bf16[8192,1024]{1,0:T(8,128)(2,1)}) %all-gather.8.cloned.1.call-update) | async-done | bytes 16777232 | tf_op jit(solution)/shard_map/all_gather | solution.py:94
  126.4 6.9 %fusion.30 = (bf16[8,1,256,1024]{3,2,1,0:T(8,128)(2,1)S(1)}, bf16[8,1,256,1024]{3,2,1,0:T(8,128)(2,1)S(1)}, bf16[8,1,256,1024]{3,2,1,0:T(8,128)(2,1)S(1)}, bf16[8,1,256,1024]{3,2,1,0:T(8,128)(2,1)S(1)}) fusion(bf16[8,4,256,1024]{3,2,1,0:T(8,128)(2,1)} %bitcast.85), kind=kLoop, calls=%fused_computation.89 | loop fusion | bytes 33554432 | tf_op jit(solution)/shard_map/slice | solution.py:95
  133.3 0.0 copy-start.15
  133.4 4.6 %fusion.5 = f32[2048,512]{1,0:T(8,128)S(1)} fusion(bf16[2048,1024]{1,0:T(8,128)(2,1)S(1)} %bitcast.88, bf16[512,4096]{1,0:T(8,128)(2,1)} %param.9), kind=kOutput, calls=%fused_computation.28 | convolution fusion | flops 2147483648 | bytes 9437184 | tf_op jit(solution)/shard_map/dot_general | solution.py:11
  138.0 1.6 copy-done.15
  139.6 2.4 fusion.7
  142.1 2.4 fusion.9
  144.5 4.6 %fusion.32 = (f32[2048]{0:T(1024)S(1)}, f32[2048,512]{1,0:T(8,128)S(1)}) fusion(bf16[2048,1024]{1,0:T(8,128)(2,1)S(1)} %bitcast.83, bf16[512,4096]{1,0:T(8,128)(2,1)} %param.9, f32[2048,512]{1,0:T(8,128)S(1)} %fusion.5, f32[2048,512]{1,0:T(8,128)S(1)} %fusion.9, f32[2048,512]{1,0:T(8,128)S(1)} %fusion.7), kind=kOutput, calls=%fused_computation.91 | convolution fusion | flops 2151675904 | bytes 22028288 | tf_op jit(solution)/shard_map/dot_general | solution.py:11
  149.1 0.0 copy-start.2
  149.1 2.0 copy-done.2
  151.1 1.6 exponential_reduce_fusion
  152.7 8.6 %all_gather.25 = f32[4,56,128]{2,1,0:T(8,128)S(1)} all-gather(f32[1,56,128]{2,1,0:T(8,128)S(1)} %fusion.26), channel_id=1, replica_groups=mesh['dp'=8,'vocab'=4] {'vocab'}, dimensions={0}, use_global_device_ids=true | all-gather | bytes 143360 | tf_op jit(solution)/shard_map/all_gather | solution.py:119
  161.5 0.1 reshape.65
  161.6 13.3 %all_gather.26 = f32[8,56,128]{2,1,0:T(8,128)S(1)} all-gather(f32[1,56,128]{2,1,0:T(8,128)S(1)} %fusion.25), channel_id=1, replica_groups=mesh['dp'=8,'vocab'=4] {'dp'}, dimensions={0}, use_global_device_ids=true | all-gather | bytes 258048 | tf_op jit(solution)/shard_map/all_gather | solution.py:119
  175.1 4.2 %multiply_convert_fusion = bf16[2048,512]{1,0:T(8,128)(2,1)S(1)} fusion(f32[2048,512]{1,0:T(8,128)} %copy-done.2, f32[2048]{0:T(1024)S(1)} %fusion.20, f32[2048]{0:T(1024)S(1)} %get-tuple-element.5, s32[2048]{0:T(1024)S(1)} %bitcast.107, f32[2048]{0:T(1024)S(1)} %bitcast.108), kind=kLoop, calls=%fused_computation.5 | loop fusion | flops 7340032 | bytes 6324224 | tf_op jit(solution)/shard_map/convert_element_type | solution.py:134
  179.3 0.2 constant_dynamic-slice_fusion.7
  179.5 6.7 %convolution_convert_fusion = bf16[1024,4096]{1,0:T(8,128)(2,1)} fusion(bf16[1024,512]{1,0:T(8,128)(2,1)S(1)} %bitcast.97, bf16[512,4096]{1,0:T(8,128)(2,1)S(1)} %copy-done.16), kind=kOutput, calls=%fused_computation.2 | convolution fusion | flops 4299161600 | bytes 13631488 | tf_op jit(solution)/shard_map/dot_general | solution.py:11
  186.3 0.3 collective-permute-start
  186.6 0.0 all-gather.6.cloned.1.call-update
  186.7 13.1 %collective-permute-done = bf16[1024,4096]{1,0:T(8,128)(2,1)} collective-permute-done((bf16[1024,4096]{1,0:T(8,128)(2,1)}, bf16[1024,4096]{1,0:T(8,128)(2,1)}, u32[]{:S(2)}, u32[]{:S(2)}) %collective-permute-start) | collective-permute-done | bytes 8388640 | tf_op jit(solution)/shard_map/ppermute | solution.py:33
  199.8 8.2 %add_convert_fusion = bf16[1024,4096]{1,0:T(8,128)(2,1)S(1)} fusion(bf16[1024,4096]{1,0:T(8,128)(2,1)} %collective-permute-done, bf16[1024,512]{1,0:T(8,128)(2,1)S(1)} %bitcast.96, bf16[512,4096]{1,0:T(8,128)(2,1)} %param.9), kind=kOutput, calls=%fused_computation | convolution fusion | flops 4307550208 | bytes 22020096 | tf_op jit(solution)/shard_map/dot_general | solution.py:11
  208.0 2.4 fusion.31
  210.4 2.0 copy-done.5
  212.4 1.5 constant_dynamic-slice_fusion.1
  213.9 0.6 collective-permute-start.3
  214.5 3.8 %constant_dynamic-slice_fusion.6 = (bf16[4,128,1024]{2,1,0:T(8,128)(2,1)S(1)}, bf16[4,128,1024]{2,1,0:T(8,128)(2,1)S(1)}, bf16[4,128,1024]{2,1,0:T(8,128)(2,1)S(1)}, bf16[4,128,1024]{2,1,0:T(8,128)(2,1)}) fusion(bf16[4,128,4096]{2,1,0:T(8,128)(2,1)} %get-tuple-element.18, s32[]{:T(128)S(6)} %select_n.96, s32[]{:T(128)S(6)} %select_n.99, s32[]{:T(128)S(6)} %select_n.98, ...), kind=kLoop, calls=%fused_computation.77 | loop fusion | bytes 8388624 | tf_op jit(solution)/shard_map/dynamic_slice | solution.py:40
  218.3 1.5 pad_maximum_fusion
  219.8 1.5 collective-permute-start.1
  221.2 6.0 %fusion.33 = f32[512,1024]{1,0:T(8,128)} fusion(bf16[2048,512]{1,0:T(8,128)(2,1)S(1)} %multiply_convert_fusion, bf16[2048,1024]{1,0:T(8,128)(2,1)} %bitcast.93), kind=kOutput, calls=%fused_computation.92 | convolution fusion | flops 2147483648 | bytes 8388608 | tf_op jit(solution)/shard_map/dot_general | solution.py:11
  227.2 3.7 fusion.34
  231.0 48.2 %collective-permute-done.3 = bf16[4,128,2048]{2,1,0:T(8,128)(2,1)} collective-permute-done((bf16[4,128,2048]{2,1,0:T(8,128)(2,1)}, bf16[4,128,2048]{2,1,0:T(8,128)(2,1)}, u32[]{:S(2)}, u32[]{:S(2)}) %collective-permute-start.3) | collective-permute-done | bytes 2097184 | tf_op jit(solution)/shard_map/ppermute | solution.py:47
  279.1 2.6 add_convert_fusion.1
  281.8 0.1 constant_dynamic-slice_fusion
  281.9 1.5 collective-permute-start.4
  283.4 2.6 add_convert_fusion.2
  286.0 0.1 constant_dynamic-slice_fusion.2
  286.1 1.0 collective-permute-start.2
  287.1 0.6 dynamic-slice_subtract_fusion
  287.7 3.7 fusion.35
  291.5 15.3 %collective-permute-done.4 = bf16[4,128,1024]{2,1,0:T(8,128)(2,1)S(1)} collective-permute-done((bf16[4,128,1024]{2,1,0:T(8,128)(2,1)S(1)}, bf16[4,128,1024]{2,1,0:T(8,128)(2,1)S(1)}, u32[]{:S(2)}, u32[]{:S(2)}) %collective-permute-start.4) | collective-permute-done | bytes 1048608 | tf_op jit(solution)/shard_map/ppermute | solution.py:51
  306.7 0.4 add_convert_fusion.3
  307.2 3.5 collective-permute-done.2
  310.7 0.4 add_convert_fusion.4
  311.1 0.1 fusion.16
  311.2 1.5 collective-permute-start.5
  312.8 2.3 collective-permute-start.6
  315.0 0.7 collective-permute-start.7
  315.7 3.7 fusion.36
  319.4 28.2 %collective-permute-done.5 = bf16[256,1024]{1,0:T(8,128)(2,1)S(1)} collective-permute-done((bf16[256,1024]{1,0:T(8,128)(2,1)S(1)}, bf16[256,1024]{1,0:T(8,128)(2,1)S(1)}, u32[]{:S(2)}, u32[]{:S(2)}) %collective-permute-start.5) | collective-permute-done | bytes 524320 | tf_op jit(solution)/shard_map/ppermute | solution.py:60
  347.6 8.9 %collective-permute-done.6 = bf16[256,1024]{1,0:T(8,128)(2,1)S(1)} collective-permute-done((bf16[256,1024]{1,0:T(8,128)(2,1)S(1)}, bf16[256,1024]{1,0:T(8,128)(2,1)S(1)}, u32[]{:S(2)}, u32[]{:S(2)}) %collective-permute-start.6) | collective-permute-done | bytes 524320 | tf_op jit(solution)/shard_map/ppermute | solution.py:60
  356.5 2.0 collective-permute-done.7
  358.6 1.2 fusion.2
  359.7 11.6 %maximum_add_fusion = f32[512,4096]{1,0:T(8,128)} fusion(f32[512,1024]{1,0:T(8,128)} %fusion.36, f32[512,1024]{1,0:T(8,128)} %fusion.35, f32[512,1024]{1,0:T(8,128)} %fusion.34, f32[512,1024]{1,0:T(8,128)} %fusion.33, bf16[1024,4096]{1,0:T(8,128)(2,1)} %all-gather.6.cloned.1.call-done, s32[1024]{0:T(1024)S(1)} %fusion.29), kind=kOutput, calls=%fused_computation.1 | convolution fusion | flops 4303880192 | bytes 25169920 | tf_op jit(solution)/shard_map/dot_general | solution.py:11
  (43 shorter events, 0.4 us)
Async XLA Ops:
  7.2 1.6 copy-start
  7.2 119.3 %all-gather.8.cloned.1.call-start = ((), (), s32[]{:S(2)}) async-start(), calls=%async_computation.1 | async-start | bytes 17301504 | tf_op jit(solution)/shard_map/all_gather | solution.py:94
  9.6 350.1 %all-gather.6.cloned.1.call-start = ((), (), s32[]{:S(2)}) async-start(), calls=%async_computation | async-start | bytes 8650752 | tf_op jit(solution)/shard_map/all_gather | solution.py:150
  133.3 4.7 %copy-start.10 = (bf16[8,1,256,1024]{3,2,1,0:T(8,128)(2,1)}, bf16[8,1,256,1024]{3,2,1,0:T(8,128)(2,1)S(1)}, u32[]{:S(2)}) copy-start(bf16[8,1,256,1024]{3,2,1,0:T(8,128)(2,1)S(1)} %get-tuple-element.14) | copy-start | bytes 12582916
  133.3 4.7 %copy-start.12 = (bf16[8,1,256,1024]{3,2,1,0:T(8,128)(2,1)}, bf16[8,1,256,1024]{3,2,1,0:T(8,128)(2,1)S(1)}, u32[]{:S(2)}) copy-start(bf16[8,1,256,1024]{3,2,1,0:T(8,128)(2,1)S(1)} %get-tuple-element.15) | copy-start | bytes 12582916
  133.3 8.7 %copy-start.14 = (bf16[8,1,256,1024]{3,2,1,0:T(8,128)(2,1)}, bf16[8,1,256,1024]{3,2,1,0:T(8,128)(2,1)S(1)}, u32[]{:S(2)}) copy-start(bf16[8,1,256,1024]{3,2,1,0:T(8,128)(2,1)S(1)} %get-tuple-element.16) | copy-start | bytes 12582916
  133.3 11.1 %copy-start.3 = (bf16[8,1,256,1024]{3,2,1,0:T(8,128)(2,1)}, bf16[8,1,256,1024]{3,2,1,0:T(8,128)(2,1)S(1)}, u32[]{:S(2)}) copy-start(bf16[8,1,256,1024]{3,2,1,0:T(8,128)(2,1)S(1)} %get-tuple-element.13) | copy-start | bytes 12582916
  133.3 6.3 %copy-start.15 = (bf16[512,4096]{1,0:T(8,128)(2,1)S(1)}, bf16[512,4096]{1,0:T(8,128)(2,1)}, u32[]{:S(2)}) copy-start(bf16[512,4096]{1,0:T(8,128)(2,1)} %param.9) | copy-start | bytes 12582916
  149.1 2.0 copy-start.2
  175.1 4.4 %copy-start.16 = (bf16[512,4096]{1,0:T(8,128)(2,1)S(1)}, bf16[512,4096]{1,0:T(8,128)(2,1)}, u32[]{:S(2)}) copy-start(bf16[512,4096]{1,0:T(8,128)(2,1)} %param.9) | copy-start | bytes 12582916
  179.3 108.4 %copy-start.7 = (bf16[2048,512]{1,0:T(8,128)(2,1)}, bf16[2048,512]{1,0:T(8,128)(2,1)S(1)}, u32[]{:S(2)}) copy-start(bf16[2048,512]{1,0:T(8,128)(2,1)S(1)} %multiply_convert_fusion) | copy-start | bytes 6291460
  186.3 13.5 %collective-permute-start = (bf16[1024,4096]{1,0:T(8,128)(2,1)}, bf16[1024,4096]{1,0:T(8,128)(2,1)}, u32[]{:S(2)}, u32[]{:S(2)}) collective-permute-start(bf16[1024,4096]{1,0:T(8,128)(2,1)} %convolution_convert_fusion), channel_id=1, source_target_pairs={{0,4},{4,0},{8,12},{12,8},{16,20},{20,16},{24,28},{28,24},{1,5},{5... | collective-permute-start | bytes 25165832 | tf_op jit(solution)/shard_map/ppermute | solution.py:33
  210.4 2.0 copy-start.5
  213.9 65.2 %collective-permute-start.3 = (bf16[4,128,2048]{2,1,0:T(8,128)(2,1)}, bf16[4,128,2048]{2,1,0:T(8,128)(2,1)}, u32[]{:S(2)}, u32[]{:S(2)}) collective-permute-start(bf16[4,128,2048]{2,1,0:T(8,128)(2,1)} %constant_dynamic-slice_fusion.1), channel_id=1, source_target_pairs={{0,2},{1,3},{2,0},{3,1},{4,6},{5,7},{6,4},{7,5},{8,10},{9,11},{10,... | collective-permute-start | bytes 6291464 | tf_op jit(solution)/shard_map/ppermute | solution.py:47
  219.8 63.6 %collective-permute-start.1 = (bf16[4,128,2048]{2,1,0:T(8,128)(2,1)}, bf16[4,128,2048]{2,1,0:T(8,128)(2,1)}, u32[]{:S(2)}, u32[]{:S(2)}) collective-permute-start(bf16[4,128,2048]{2,1,0:T(8,128)(2,1)} %pad_maximum_fusion), channel_id=1, source_target_pairs={{0,1},{1,0},{2,3},{3,2},{4,5},{5,4},{6,7},{7,6},{8,9},{9,8},{10,11... | collective-permute-start | bytes 6291464 | tf_op jit(solution)/shard_map/ppermute | solution.py:46
  221.2 6.0 %copy-start.13 = (bf16[8,1,256,1024]{3,2,1,0:T(8,128)(2,1)S(1)}, bf16[8,1,256,1024]{3,2,1,0:T(8,128)(2,1)}, u32[]{:S(2)}) copy-start(bf16[8,1,256,1024]{3,2,1,0:T(8,128)(2,1)} %copy-done.12) | copy-start | bytes 12582916
  227.2 51.9 %copy-start.6 = (bf16[4,128,4096]{2,1,0:T(8,128)(2,1)S(1)}, bf16[4,128,4096]{2,1,0:T(8,128)(2,1)}, u32[]{:S(2)}) copy-start(bf16[4,128,4096]{2,1,0:T(8,128)(2,1)} %copy-done.5) | copy-start | bytes 12582916
  231.0 52.4 %copy-start.9 = (bf16[4,128,1024]{2,1,0:T(8,128)(2,1)S(1)}, bf16[4,128,1024]{2,1,0:T(8,128)(2,1)}, u32[]{:S(2)}) copy-start(bf16[4,128,1024]{2,1,0:T(8,128)(2,1)} %get-tuple-element.22) | copy-start | bytes 3145732
  281.9 24.9 %collective-permute-start.4 = (bf16[4,128,1024]{2,1,0:T(8,128)(2,1)S(1)}, bf16[4,128,1024]{2,1,0:T(8,128)(2,1)S(1)}, u32[]{:S(2)}, u32[]{:S(2)}) collective-permute-start(bf16[4,128,1024]{2,1,0:T(8,128)(2,1)S(1)} %constant_dynamic-slice_fusion), channel_id=1, source_target_pairs={{0,1},{1,0},{2,3},{3,2},{4,5},{5,4},{6,7},{7,6},{8,9},{9,8},{10,11... | collective-permute-start | bytes 3145736 | tf_op jit(solution)/shard_map/ppermute | solution.py:51
  283.4 4.3 %copy-start.11 = (bf16[8,1,256,1024]{3,2,1,0:T(8,128)(2,1)S(1)}, bf16[8,1,256,1024]{3,2,1,0:T(8,128)(2,1)}, u32[]{:S(2)}) copy-start(bf16[8,1,256,1024]{3,2,1,0:T(8,128)(2,1)} %copy-done.10) | copy-start | bytes 12582916
  286.1 24.6 %collective-permute-start.2 = (bf16[4,128,1024]{2,1,0:T(8,128)(2,1)S(1)}, bf16[4,128,1024]{2,1,0:T(8,128)(2,1)S(1)}, u32[]{:S(2)}, u32[]{:S(2)}) collective-permute-start(bf16[4,128,1024]{2,1,0:T(8,128)(2,1)S(1)} %constant_dynamic-slice_fusion.2), channel_id=1, source_target_pairs={{0,2},{1,3},{2,0},{3,1},{4,6},{5,7},{6,4},{7,5},{8,10},{9,11},{10,... | collective-permute-start | bytes 3145736 | tf_op jit(solution)/shard_map/ppermute | solution.py:50
  307.1 8.6 %copy-start.4 = (bf16[8,1,256,1024]{3,2,1,0:T(8,128)(2,1)S(1)}, bf16[8,1,256,1024]{3,2,1,0:T(8,128)(2,1)}, u32[]{:S(2)}) copy-start(bf16[8,1,256,1024]{3,2,1,0:T(8,128)(2,1)} %copy-done.3) | copy-start | bytes 12582916
  307.2 8.6 %copy-start.8 = (bf16[2048,512]{1,0:T(8,128)(2,1)S(1)}, bf16[2048,512]{1,0:T(8,128)(2,1)}, u32[]{:S(2)}) copy-start(bf16[2048,512]{1,0:T(8,128)(2,1)} %copy-done.7) | copy-start | bytes 6291460
  311.2 36.4 %collective-permute-start.5 = (bf16[256,1024]{1,0:T(8,128)(2,1)S(1)}, bf16[256,1024]{1,0:T(8,128)(2,1)S(1)}, u32[]{:S(2)}, u32[]{:S(2)}) collective-permute-start(bf16[256,1024]{1,0:T(8,128)(2,1)S(1)} %get-tuple-element.23), channel_id=1, source_target_pairs={{0,8},{4,12},{8,16},{12,20},{16,24},{20,28},{24,0},{28,4},{1,9},{5... | collective-permute-start | bytes 1572872 | tf_op jit(solution)/shard_map/ppermute | solution.py:60
  312.8 43.7 %collective-permute-start.6 = (bf16[256,1024]{1,0:T(8,128)(2,1)S(1)}, bf16[256,1024]{1,0:T(8,128)(2,1)S(1)}, u32[]{:S(2)}, u32[]{:S(2)}) collective-permute-start(bf16[256,1024]{1,0:T(8,128)(2,1)S(1)} %get-tuple-element.24), channel_id=1, source_target_pairs={{0,16},{4,20},{8,24},{12,28},{16,0},{20,4},{24,8},{28,12},{1,17},{... | collective-permute-start | bytes 1572872 | tf_op jit(solution)/shard_map/ppermute | solution.py:60
  315.0 43.5 %collective-permute-start.7 = (bf16[256,1024]{1,0:T(8,128)(2,1)S(1)}, bf16[256,1024]{1,0:T(8,128)(2,1)S(1)}, u32[]{:S(2)}, u32[]{:S(2)}) collective-permute-start(bf16[256,1024]{1,0:T(8,128)(2,1)S(1)} %get-tuple-element.25), channel_id=1, source_target_pairs={{0,24},{4,28},{8,0},{12,4},{16,8},{20,12},{24,16},{28,20},{1,25},{... | collective-permute-start | bytes 1572872 | tf_op jit(solution)/shard_map/ppermute | solution.py:60
  359.7 11.6 %copy-start.1 = (bf16[256,4096]{1,0:T(8,128)(2,1)S(1)}, bf16[256,4096]{1,0:T(8,128)(2,1)}, u32[]{:S(2)}) copy-start(bf16[256,4096]{1,0:T(8,128)(2,1)} %param.8) | copy-start | bytes 6291460
Sparse Core Ops, SparseCore 0:
  11.5 114.9 all-gather.7
  186.8 94.0 all-gather.5
